TPU v7x, 128 devices: a whole 4x4x4 slice. The times are simulated.
128 devices in a mesh: tok: 8 (over x, core), feat: 16 (over z, y).
Axes of the slice: x: 4, y: 4, z: 4, core: 2. Of those that a mesh axis runs over, the one named last changes fastest.
Arguments:
- activations: bfloat16 [8192, 28672], P('tok', 'feat'), may hold values from -6 to 6
- out_grads: bfloat16 [8192, 8192], P('tok', 'feat'), may hold values from -6 to 6
- query_out: bfloat16 [64, 32, 8192], P('tok', None, 'feat'), may hold values from -0.0625 to 0.0625
- query_in: bfloat16 [64, 32, 28672], P('tok', None, 'feat'), may hold values from -0.03125 to 0.03125
Outputs:
- influence: float32 [8192, 64], P(('tok', 'feat'))
All inputs are finite; a program needn't handle non-finite values.
Results may differ from a plain program's by a relative error of at most 0.0003.
Values may be sent and summed in bfloat16 or wider, within the bound.
A program may use at most 128 MiB of HBM per device.

v0:
```python
import jax
import jax.numpy as jnp
from jax import lax
from jax.sharding import PartitionSpec as P

RANK = 32


def passed_along(value, axis, steps):
    count = lax.axis_size(axis)
    pairs = [(source, (source + steps) % count) for source in range(count)]
    return lax.ppermute(value, axis, pairs)


def project(out_grads, activations, outer, inner):
    count = outer.shape[0] * outer.shape[1]
    flat_outer = outer.reshape(count, outer.shape[2])
    flat_inner = inner.reshape(count, inner.shape[2])
    grad_proj = jnp.einsum("td,cd->tc", out_grads, flat_outer, preferred_element_type=jnp.float32)
    act_proj = jnp.einsum("tf,cf->tc", activations, flat_inner, preferred_element_type=jnp.float32)
    return (grad_proj, act_proj)


def combine_rank(grad_proj, act_proj):
    rows = grad_proj.shape[0]
    product = (grad_proj * act_proj).reshape(rows, grad_proj.shape[1] // RANK, RANK)
    return jnp.sum(product, axis=2) * RANK ** (-0.5)


def block_scores(out_grads, activations, outer, inner):
    grad_proj, act_proj = project(out_grads, activations, outer, inner)
    grad_proj, act_proj = (
        lax.psum_scatter(grad_proj, "feat", scatter_dimension=0, tiled=True),
        lax.psum_scatter(act_proj, "feat", scatter_dimension=0, tiled=True),
    )
    return combine_rank(grad_proj, act_proj)


def shards(activations, out_grads, query_out, query_in):
    tok_rows = activations.shape[0]
    cycle_size = lax.axis_size("tok")
    share_rows = tok_rows // lax.axis_size("feat")
    per_block = query_out.shape[0]
    position = lax.axis_index("tok")
    scores = jnp.zeros((share_rows, cycle_size * per_block), jnp.float32)
    first = block_scores(out_grads, activations, query_out, query_in)
    scores = lax.dynamic_update_slice(scores, first, (jnp.int32(0), position * per_block))

    def advance(turn, carry):
        blocks, totals = carry
        blocks = passed_along((blocks[0], blocks[1]), "tok", 1)
        owner = (position - turn) % cycle_size
        fresh = block_scores(out_grads, activations, blocks[0], blocks[1])
        totals = lax.dynamic_update_slice(totals, fresh, (jnp.int32(0), owner * per_block))
        return (blocks, totals)

    blocks_end, scores = lax.fori_loop(1, cycle_size, advance, ((query_out, query_in), scores))
    return scores


def solution(mesh):
    return jax.shard_map(
        shards,
        mesh=mesh,
        in_specs=(
            P("tok", "feat"),
            P("tok", "feat"),
            P("tok", None, "feat"),
            P("tok", None, "feat"),
        ),
        out_specs=P(("tok", "feat"), None),
        check_vma=False,
    )
```

profile of v0, /device:TPU:0, one launch (start us, length us, event | category | flops | bytes accessed | tf_op | source)
XLA Modules:
  0.0 1268.8 jit_solution(3355986989255766762)
XLA Ops:
  6.5 1.2 copy.29
  7.7 0.9 copy.28
  8.7 4.3 fusion.3
  13.0 1.5 fusion.2
  14.5 74.1 %reduce-scatter.7.cloned.1.call-done = f32[64,256]{1,0:T(8,128)} async-done(((f32[1024,256]{1,0:T(8,128)}), f32[64,256]{1,0:T(8,128)}) %reduce-scatter.7.cloned.1.call-update) | async-done | bytes 65552 | tf_op jit(solution)/shard_map/reduce_scatter | solution.py:34
  88.7 75.8 %reduce-scatter.5.cloned.1.call-done = f32[64,256]{1,0:T(8,128)} async-done(((f32[1024,256]{1,0:T(8,128)}), f32[64,256]{1,0:T(8,128)}) %reduce-scatter.5.cloned.1.call-update) | async-done | bytes 65552 | tf_op jit(solution)/shard_map/reduce_scatter | solution.py:33
  164.5 0.9 mul.39
  165.4 0.1 copy.8
  165.5 1096.0 %while.19 = (s32[]{:T(128)}, bf16[8,32,512]{2,1,0:T(8,128)(2,1)S(1)}, bf16[8,32,1792]{2,1,0:T(8,128)(2,1)S(1)}, f32[64,64]{0,1:T(8,128)S(1)}, bf16[1024,512]{1,0...) while((s32[]{:T(128)}, ...), condition=%wide.region_7.8_spmd, body=%wide.region_3.7_spmd.sunk | while | flops 1207992320 | bytes 22161856 | solution.py:57
  165.6 7.0 collective-permute-done
  172.6 1.5 fusion.22
  174.2 14.0 %collective-permute-done.1 = bf16[8,32,1792]{2,1,0:T(8,128)(2,1)S(1)} collective-permute-done((bf16[8,32,1792]{2,1,0:T(8,128)(2,1)S(1)}, bf16[8,32,1792]{2,1,0:T(8,128)(2,1)S(1)}, u32[]{:S(2)}, u32[]{:S(2)}) %collective-permute-start.1) | collective-permute-done | bytes 917536 | tf_op jit(solution)/shard_map/while/body/eval_jaxpr/ppermute | solution.py:12
  188.2 4.2 fusion.23
  192.6 52.8 %reduce-scatter.9.cloned.1.call-done = f32[64,256]{1,0:T(8,128)} async-done(((f32[1024,256]{1,0:T(8,128)}), f32[64,256]{1,0:T(8,128)}) %reduce-scatter.9.cloned.1.call-update) | async-done | bytes 65552 | tf_op jit(solution)/shard_map/while/body/eval_jaxpr/reduce_scatter | solution.py:33
  245.4 75.7 %reduce-scatter.11.cloned.1.call-done = f32[64,256]{1,0:T(8,128)} async-done(((f32[1024,256]{1,0:T(8,128)}), f32[64,256]{1,0:T(8,128)}) %reduce-scatter.11.cloned.1.call-update) | async-done | bytes 65552 | tf_op jit(solution)/shard_map/while/body/eval_jaxpr/reduce_scatter | solution.py:34
  321.1 0.9 mul.49
  322.0 0.1 copy.11
  322.2 7.0 collective-permute-done
  329.2 1.5 fusion.22
  330.8 14.0 %collective-permute-done.1 = bf16[8,32,1792]{2,1,0:T(8,128)(2,1)S(1)} collective-permute-done((bf16[8,32,1792]{2,1,0:T(8,128)(2,1)S(1)}, bf16[8,32,1792]{2,1,0:T(8,128)(2,1)S(1)}, u32[]{:S(2)}, u32[]{:S(2)}) %collective-permute-start.1) | collective-permute-done | bytes 917536 | tf_op jit(solution)/shard_map/while/body/eval_jaxpr/ppermute | solution.py:12
  344.8 4.2 fusion.23
  349.1 52.8 %reduce-scatter.9.cloned.1.call-done = f32[64,256]{1,0:T(8,128)} async-done(((f32[1024,256]{1,0:T(8,128)}), f32[64,256]{1,0:T(8,128)}) %reduce-scatter.9.cloned.1.call-update) | async-done | bytes 65552 | tf_op jit(solution)/shard_map/while/body/eval_jaxpr/reduce_scatter | solution.py:33
  401.9 75.7 %reduce-scatter.11.cloned.1.call-done = f32[64,256]{1,0:T(8,128)} async-done(((f32[1024,256]{1,0:T(8,128)}), f32[64,256]{1,0:T(8,128)}) %reduce-scatter.11.cloned.1.call-update) | async-done | bytes 65552 | tf_op jit(solution)/shard_map/while/body/eval_jaxpr/reduce_scatter | solution.py:34
  477.6 0.9 mul.49
  478.5 0.1 copy.11
  478.8 7.0 collective-permute-done
  485.7 1.5 fusion.22
  487.3 14.0 %collective-permute-done.1 = bf16[8,32,1792]{2,1,0:T(8,128)(2,1)S(1)} collective-permute-done((bf16[8,32,1792]{2,1,0:T(8,128)(2,1)S(1)}, bf16[8,32,1792]{2,1,0:T(8,128)(2,1)S(1)}, u32[]{:S(2)}, u32[]{:S(2)}) %collective-permute-start.1) | collective-permute-done | bytes 917536 | tf_op jit(solution)/shard_map/while/body/eval_jaxpr/ppermute | solution.py:12
  501.3 4.2 fusion.23
  505.7 52.7 %reduce-scatter.9.cloned.1.call-done = f32[64,256]{1,0:T(8,128)} async-done(((f32[1024,256]{1,0:T(8,128)}), f32[64,256]{1,0:T(8,128)}) %reduce-scatter.9.cloned.1.call-update) | async-done | bytes 65552 | tf_op jit(solution)/shard_map/while/body/eval_jaxpr/reduce_scatter | solution.py:33
  558.4 75.8 %reduce-scatter.11.cloned.1.call-done = f32[64,256]{1,0:T(8,128)} async-done(((f32[1024,256]{1,0:T(8,128)}), f32[64,256]{1,0:T(8,128)}) %reduce-scatter.11.cloned.1.call-update) | async-done | bytes 65552 | tf_op jit(solution)/shard_map/while/body/eval_jaxpr/reduce_scatter | solution.py:34
  634.2 0.9 mul.49
  635.1 0.1 copy.11
  635.3 7.0 collective-permute-done
  642.3 1.5 fusion.22
  643.9 14.0 %collective-permute-done.1 = bf16[8,32,1792]{2,1,0:T(8,128)(2,1)S(1)} collective-permute-done((bf16[8,32,1792]{2,1,0:T(8,128)(2,1)S(1)}, bf16[8,32,1792]{2,1,0:T(8,128)(2,1)S(1)}, u32[]{:S(2)}, u32[]{:S(2)}) %collective-permute-start.1) | collective-permute-done | bytes 917536 | tf_op jit(solution)/shard_map/while/body/eval_jaxpr/ppermute | solution.py:12
  657.9 4.2 fusion.23
  662.3 52.8 %reduce-scatter.9.cloned.1.call-done = f32[64,256]{1,0:T(8,128)} async-done(((f32[1024,256]{1,0:T(8,128)}), f32[64,256]{1,0:T(8,128)}) %reduce-scatter.9.cloned.1.call-update) | async-done | bytes 65552 | tf_op jit(solution)/shard_map/while/body/eval_jaxpr/reduce_scatter | solution.py:33
  715.0 75.7 %reduce-scatter.11.cloned.1.call-done = f32[64,256]{1,0:T(8,128)} async-done(((f32[1024,256]{1,0:T(8,128)}), f32[64,256]{1,0:T(8,128)}) %reduce-scatter.11.cloned.1.call-update) | async-done | bytes 65552 | tf_op jit(solution)/shard_map/while/body/eval_jaxpr/reduce_scatter | solution.py:34
  790.7 0.9 mul.49
  791.6 0.1 copy.11
  791.9 7.0 collective-permute-done
  798.9 1.5 fusion.22
  800.4 14.0 %collective-permute-done.1 = bf16[8,32,1792]{2,1,0:T(8,128)(2,1)S(1)} collective-permute-done((bf16[8,32,1792]{2,1,0:T(8,128)(2,1)S(1)}, bf16[8,32,1792]{2,1,0:T(8,128)(2,1)S(1)}, u32[]{:S(2)}, u32[]{:S(2)}) %collective-permute-start.1) | collective-permute-done | bytes 917536 | tf_op jit(solution)/shard_map/while/body/eval_jaxpr/ppermute | solution.py:12
  814.4 4.2 fusion.23
  818.8 52.8 %reduce-scatter.9.cloned.1.call-done = f32[64,256]{1,0:T(8,128)} async-done(((f32[1024,256]{1,0:T(8,128)}), f32[64,256]{1,0:T(8,128)}) %reduce-scatter.9.cloned.1.call-update) | async-done | bytes 65552 | tf_op jit(solution)/shard_map/while/body/eval_jaxpr/reduce_scatter | solution.py:33
  871.6 75.7 %reduce-scatter.11.cloned.1.call-done = f32[64,256]{1,0:T(8,128)} async-done(((f32[1024,256]{1,0:T(8,128)}), f32[64,256]{1,0:T(8,128)}) %reduce-scatter.11.cloned.1.call-update) | async-done | bytes 65552 | tf_op jit(solution)/shard_map/while/body/eval_jaxpr/reduce_scatter | solution.py:34
  947.3 0.9 mul.49
  948.2 0.1 copy.11
  948.4 7.0 collective-permute-done
  955.4 1.5 fusion.22
  957.0 14.0 %collective-permute-done.1 = bf16[8,32,1792]{2,1,0:T(8,128)(2,1)S(1)} collective-permute-done((bf16[8,32,1792]{2,1,0:T(8,128)(2,1)S(1)}, bf16[8,32,1792]{2,1,0:T(8,128)(2,1)S(1)}, u32[]{:S(2)}, u32[]{:S(2)}) %collective-permute-start.1) | collective-permute-done | bytes 917536 | tf_op jit(solution)/shard_map/while/body/eval_jaxpr/ppermute | solution.py:12
  971.0 4.2 fusion.23
  975.4 52.8 %reduce-scatter.9.cloned.1.call-done = f32[64,256]{1,0:T(8,128)} async-done(((f32[1024,256]{1,0:T(8,128)}), f32[64,256]{1,0:T(8,128)}) %reduce-scatter.9.cloned.1.call-update) | async-done | bytes 65552 | tf_op jit(solution)/shard_map/while/body/eval_jaxpr/reduce_scatter | solution.py:33
  1028.2 75.8 %reduce-scatter.11.cloned.1.call-done = f32[64,256]{1,0:T(8,128)} async-done(((f32[1024,256]{1,0:T(8,128)}), f32[64,256]{1,0:T(8,128)}) %reduce-scatter.11.cloned.1.call-update) | async-done | bytes 65552 | tf_op jit(solution)/shard_map/while/body/eval_jaxpr/reduce_scatter | solution.py:34
  1104.0 0.9 mul.49
  1105.1 7.0 collective-permute-done
  1112.1 1.5 fusion.22
  1113.6 14.0 %collective-permute-done.1 = bf16[8,32,1792]{2,1,0:T(8,128)(2,1)S(1)} collective-permute-done((bf16[8,32,1792]{2,1,0:T(8,128)(2,1)S(1)}, bf16[8,32,1792]{2,1,0:T(8,128)(2,1)S(1)}, u32[]{:S(2)}, u32[]{:S(2)}) %collective-permute-start.1) | collective-permute-done | bytes 917536 | tf_op jit(solution)/shard_map/while/body/eval_jaxpr/ppermute | solution.py:12
  1127.7 4.2 fusion.23
  1132.0 52.8 %reduce-scatter.9.cloned.1.call-done = f32[64,256]{1,0:T(8,128)} async-done(((f32[1024,256]{1,0:T(8,128)}), f32[64,256]{1,0:T(8,128)}) %reduce-scatter.9.cloned.1.call-update) | async-done | bytes 65552 | tf_op jit(solution)/shard_map/while/body/eval_jaxpr/reduce_scatter | solution.py:33
  1184.8 75.7 %reduce-scatter.11.cloned.1.call-done = f32[64,256]{1,0:T(8,128)} async-done(((f32[1024,256]{1,0:T(8,128)}), f32[64,256]{1,0:T(8,128)}) %reduce-scatter.11.cloned.1.call-update) | async-done | bytes 65552 | tf_op jit(solution)/shard_map/while/body/eval_jaxpr/reduce_scatter | solution.py:34
  1260.6 0.9 mul.49
  1261.6 0.7 copy.9
  (81 shorter events, 2.1 us)
Async XLA Ops:
  6.5 82.2 %reduce-scatter.7.cloned.1.call-start = ((), (), s32[]{:S(2)}) async-start(), calls=%async_computation.5 | async-start | bytes 1114112 | tf_op jit(solution)/shard_map/reduce_scatter | solution.py:34
  8.7 4.3 copy-start
  13.0 151.6 %reduce-scatter.5.cloned.1.call-start = ((), (), s32[]{:S(2)}) async-start(), calls=%async_computation.4 | async-start | bytes 1114112 | tf_op jit(solution)/shard_map/reduce_scatter | solution.py:33
  165.6 79.8 %reduce-scatter.9.cloned.1.call-start = ((), (), s32[]{:S(2)}) async-start(), calls=%async_computation.6 | async-start | bytes 1114112 | tf_op jit(solution)/shard_map/while/body/eval_jaxpr/reduce_scatter | solution.py:33
  165.6 7.0 collective-permute-start
  174.1 147.0 %reduce-scatter.11.cloned.1.call-start = ((), (), s32[]{:S(2)}) async-start(), calls=%async_computation.7 | async-start | bytes 1114112 | tf_op jit(solution)/shard_map/while/body/eval_jaxpr/reduce_scatter | solution.py:34
  174.2 14.0 %collective-permute-start.1 = (bf16[8,32,1792]{2,1,0:T(8,128)(2,1)S(1)}, bf16[8,32,1792]{2,1,0:T(8,128)(2,1)S(1)}, u32[]{:S(2)}, u32[]{:S(2)}) collective-permute-start(bf16[8,32,1792]{2,1,0:T(8,128)(2,1)S(1)} %get-tuple-element.254), channel_id=1, source_target_pairs={{0,16},{16,32},{32,48},{48,64},{64,80},{80,96},{96,112},{112,0},{1... | collective-permute-start | bytes 2752520 | tf_op jit(solution)/shard_map/while/body/eval_jaxpr/ppermute | solution.py:12
  322.1 79.8 %reduce-scatter.9.cloned.1.call-start = ((), (), s32[]{:S(2)}) async-start(), calls=%async_computation.6 | async-start | bytes 1114112 | tf_op jit(solution)/shard_map/while/body/eval_jaxpr/reduce_scatter | solution.py:33
  322.2 7.0 collective-permute-start
  330.7 147.0 %reduce-scatter.11.cloned.1.call-start = ((), (), s32[]{:S(2)}) async-start(), calls=%async_computation.7 | async-start | bytes 1114112 | tf_op jit(solution)/shard_map/while/body/eval_jaxpr/reduce_scatter | solution.py:34
  330.7 14.0 %collective-permute-start.1 = (bf16[8,32,1792]{2,1,0:T(8,128)(2,1)S(1)}, bf16[8,32,1792]{2,1,0:T(8,128)(2,1)S(1)}, u32[]{:S(2)}, u32[]{:S(2)}) collective-permute-start(bf16[8,32,1792]{2,1,0:T(8,128)(2,1)S(1)} %get-tuple-element.254), channel_id=1, source_target_pairs={{0,16},{16,32},{32,48},{48,64},{64,80},{80,96},{96,112},{112,0},{1... | collective-permute-start | bytes 2752520 | tf_op jit(solution)/shard_map/while/body/eval_jaxpr/ppermute | solution.py:12
  478.7 79.8 %reduce-scatter.9.cloned.1.call-start = ((), (), s32[]{:S(2)}) async-start(), calls=%async_computation.6 | async-start | bytes 1114112 | tf_op jit(solution)/shard_map/while/body/eval_jaxpr/reduce_scatter | solution.py:33
  478.7 7.0 collective-permute-start
  487.2 147.0 %reduce-scatter.11.cloned.1.call-start = ((), (), s32[]{:S(2)}) async-start(), calls=%async_computation.7 | async-start | bytes 1114112 | tf_op jit(solution)/shard_map/while/body/eval_jaxpr/reduce_scatter | solution.py:34
  487.3 14.0 %collective-permute-start.1 = (bf16[8,32,1792]{2,1,0:T(8,128)(2,1)S(1)}, bf16[8,32,1792]{2,1,0:T(8,128)(2,1)S(1)}, u32[]{:S(2)}, u32[]{:S(2)}) collective-permute-start(bf16[8,32,1792]{2,1,0:T(8,128)(2,1)S(1)} %get-tuple-element.254), channel_id=1, source_target_pairs={{0,16},{16,32},{32,48},{48,64},{64,80},{80,96},{96,112},{112,0},{1... | collective-permute-start | bytes 2752520 | tf_op jit(solution)/shard_map/while/body/eval_jaxpr/ppermute | solution.py:12
  635.3 79.8 %reduce-scatter.9.cloned.1.call-start = ((), (), s32[]{:S(2)}) async-start(), calls=%async_computation.6 | async-start | bytes 1114112 | tf_op jit(solution)/shard_map/while/body/eval_jaxpr/reduce_scatter | solution.py:33
  635.3 7.0 collective-permute-start
  643.8 146.9 %reduce-scatter.11.cloned.1.call-start = ((), (), s32[]{:S(2)}) async-start(), calls=%async_computation.7 | async-start | bytes 1114112 | tf_op jit(solution)/shard_map/while/body/eval_jaxpr/reduce_scatter | solution.py:34
  643.9 14.0 %collective-permute-start.1 = (bf16[8,32,1792]{2,1,0:T(8,128)(2,1)S(1)}, bf16[8,32,1792]{2,1,0:T(8,128)(2,1)S(1)}, u32[]{:S(2)}, u32[]{:S(2)}) collective-permute-start(bf16[8,32,1792]{2,1,0:T(8,128)(2,1)S(1)} %get-tuple-element.254), channel_id=1, source_target_pairs={{0,16},{16,32},{32,48},{48,64},{64,80},{80,96},{96,112},{112,0},{1... | collective-permute-start | bytes 2752520 | tf_op jit(solution)/shard_map/while/body/eval_jaxpr/ppermute | solution.py:12
  791.8 79.8 %reduce-scatter.9.cloned.1.call-start = ((), (), s32[]{:S(2)}) async-start(), calls=%async_computation.6 | async-start | bytes 1114112 | tf_op jit(solution)/shard_map/while/body/eval_jaxpr/reduce_scatter | solution.py:33
  791.8 7.0 collective-permute-start
  800.3 147.0 %reduce-scatter.11.cloned.1.call-start = ((), (), s32[]{:S(2)}) async-start(), calls=%async_computation.7 | async-start | bytes 1114112 | tf_op jit(solution)/shard_map/while/body/eval_jaxpr/reduce_scatter | solution.py:34
  800.4 14.0 %collective-permute-start.1 = (bf16[8,32,1792]{2,1,0:T(8,128)(2,1)S(1)}, bf16[8,32,1792]{2,1,0:T(8,128)(2,1)S(1)}, u32[]{:S(2)}, u32[]{:S(2)}) collective-permute-start(bf16[8,32,1792]{2,1,0:T(8,128)(2,1)S(1)} %get-tuple-element.254), channel_id=1, source_target_pairs={{0,16},{16,32},{32,48},{48,64},{64,80},{80,96},{96,112},{112,0},{1... | collective-permute-start | bytes 2752520 | tf_op jit(solution)/shard_map/while/body/eval_jaxpr/ppermute | solution.py:12
  948.4 79.8 %reduce-scatter.9.cloned.1.call-start = ((), (), s32[]{:S(2)}) async-start(), calls=%async_computation.6 | async-start | bytes 1114112 | tf_op jit(solution)/shard_map/while/body/eval_jaxpr/reduce_scatter | solution.py:33
  948.4 7.0 collective-permute-start
  956.9 147.1 %reduce-scatter.11.cloned.1.call-start = ((), (), s32[]{:S(2)}) async-start(), calls=%async_computation.7 | async-start | bytes 1114112 | tf_op jit(solution)/shard_map/while/body/eval_jaxpr/reduce_scatter | solution.py:34
  957.0 14.0 %collective-permute-start.1 = (bf16[8,32,1792]{2,1,0:T(8,128)(2,1)S(1)}, bf16[8,32,1792]{2,1,0:T(8,128)(2,1)S(1)}, u32[]{:S(2)}, u32[]{:S(2)}) collective-permute-start(bf16[8,32,1792]{2,1,0:T(8,128)(2,1)S(1)} %get-tuple-element.254), channel_id=1, source_target_pairs={{0,16},{16,32},{32,48},{48,64},{64,80},{80,96},{96,112},{112,0},{1... | collective-permute-start | bytes 2752520 | tf_op jit(solution)/shard_map/while/body/eval_jaxpr/ppermute | solution.py:12
  1105.0 79.8 %reduce-scatter.9.cloned.1.call-start = ((), (), s32[]{:S(2)}) async-start(), calls=%async_computation.6 | async-start | bytes 1114112 | tf_op jit(solution)/shard_map/while/body/eval_jaxpr/reduce_scatter | solution.py:33
  1105.1 7.0 collective-permute-start
  1113.6 147.0 %reduce-scatter.11.cloned.1.call-start = ((), (), s32[]{:S(2)}) async-start(), calls=%async_computation.7 | async-start | bytes 1114112 | tf_op jit(solution)/shard_map/while/body/eval_jaxpr/reduce_scatter | solution.py:34
  1113.6 14.0 %collective-permute-start.1 = (bf16[8,32,1792]{2,1,0:T(8,128)(2,1)S(1)}, bf16[8,32,1792]{2,1,0:T(8,128)(2,1)S(1)}, u32[]{:S(2)}, u32[]{:S(2)}) collective-permute-start(bf16[8,32,1792]{2,1,0:T(8,128)(2,1)S(1)} %get-tuple-element.254), channel_id=1, source_target_pairs={{0,16},{16,32},{32,48},{48,64},{64,80},{80,96},{96,112},{112,0},{1... | collective-permute-start | bytes 2752520 | tf_op jit(solution)/shard_map/while/body/eval_jaxpr/ppermute | solution.py:12
Sparse Core Ops, SparseCore 0:
  13.1 75.5 reduce-scatter.6
  92.2 72.2 reduce-scatter.4
  174.2 71.0 reduce-scatter.8
  248.8 72.2 reduce-scatter.10
  330.8 71.0 reduce-scatter.8
  405.3 72.2 reduce-scatter.10
  487.4 71.0 reduce-scatter.8
  562.0 72.2 reduce-scatter.10
  643.9 71.0 reduce-scatter.8
  718.4 72.2 reduce-scatter.10
  800.5 71.0 reduce-scatter.8
  875.0 72.2 reduce-scatter.10
  957.0 71.1 reduce-scatter.8
  1031.6 72.3 reduce-scatter.10
  1113.7 71.1 reduce-scatter.8
  1188.2 72.2 reduce-scatter.10
where the time goes:
time: 1270 us
  waiting for transfers between devices  1200 us (94%)
  matrix products  45.5 us (4%)
  between operations  13.1 us (1%)
    reduce_scatter x8, waiting for transfers between devices, block_scores(): lax.psum_scatter(act_proj, 'feat', scatter_dimension=0, tiled=True)  604 us
    reduce_scatter x8, waiting for transfers between devices, block_scores(): lax.psum_scatter(grad_proj, 'feat', scatter_dimension=0, tiled=True)  445 us
    ppermute x14, waiting for transfers between devices, passed_along(): return lax.ppermute(value, axis, pairs)  147 us
    dot_general x8, matrix products, project(): jnp.einsum('tf,cf->tc', activations, flat_inner, preferred_element_type=j...  33.8 us
  transfers between devices with their start and end apart: 30, of which 30 were waited for; matrix products, arithmetic and copies ran while one was open for 2% of the time, Pallas kernels for 0%

commit v1 on v0

v1 whole, which is shorter than its diff:
```python
import jax
import jax.numpy as jnp
from jax import lax
from jax.experimental import pallas as pl
from jax.experimental.pallas import tpu as pltpu
from jax.sharding import PartitionSpec as P

RANK = 32
MESH = pl.DeviceIdType.MESH
F32 = jnp.float32
BF16 = jnp.bfloat16

STREAMS = 4
LEVELS = 4
STEPS = 8
SLOTS = 5
POWER = 17
TOP = 2.0 ** (127.0 / POWER)
TINY = 2.0**-100
IDLE = (2,)
TURNS = STEPS + len(IDLE) + LEVELS
NEAR_A, NEAR_B, FAR = (2, 5), (3, 6), (4, 7)


def flip_one(v):
    return v + 1 - 2 * (v % 2)


def flip_three(v):
    return 3 - v


def encode(value, inverse):
    n = value * inverse
    n2 = n * n
    n4 = n2 * n2
    n8 = n4 * n4
    return (n8 * n8 * n).astype(BF16)


def decode(sent, scale):
    y = sent.astype(F32)
    log = jnp.log2(jnp.maximum(jnp.abs(y), 2.0**-126))
    return y * jnp.exp2(log * (1.0 / POWER - 1.0)) * scale


def bound_above(bound):
    return jnp.maximum((bound * 1.01).astype(BF16).astype(F32), TINY)


def tiles(value):
    return value.reshape(value.shape[0] // 8, 8, 128)


def rows_of(value):
    return value.reshape(value.shape[0] * 8, 128)


def kernel(
    act, og, qi, qo, out,
    a_v, g_v, qi_v, qo_v, part, bounds, prod,
    s1, s2, s3, s4, r1, r2, r3, r4,
    load_sem, own_sem, q_send, q_recv, m_send, m_recv,
):
    tok = lax.axis_index("tok")
    feat = lax.axis_index("feat")
    x, core = tok // 2, tok % 2
    z, y = feat // 4, feat % 4
    sibling = (tok + 1 - 2 * core, feat)
    near_a = (flip_one(x) * 2 + core, feat)
    near_b = (flip_three(x) * 2 + core, feat)
    partners = (
        (tok, z * 4 + flip_one(y)),
        (tok, z * 4 + flip_three(y)),
        (tok, flip_one(z) * 4 + y),
        (tok, flip_three(z) * 4 + y),
    )
    sends, recvs = (s1, s2, s3, s4), (r1, r2, r3, r4)

    own = []
    for h in range(2):
        for a, (src, dst) in enumerate(((qi, qi_v), (qo, qo_v))):
            copy = pltpu.make_async_copy(src.at[pl.ds(h * 128, 128)], dst.at[h, core], own_sem.at[a, h])
            copy.start()
            own.append(copy)

    def load(n, carry):
        half = 1 - n // 32
        k = (n // 8) % 4
        position = (1 - n // 32) * 8 + n % 8
        bits = [(position // 8) % 2, (position // 4) % 2, (position // 2) % 2, position % 2]
        flips = []
        for d in range(4):
            j = (d - k + 4) % 4
            flips.append((position // (8 // (1 + j % 2 + (j // 2) * 3 + (j // 2) * (j % 2) * 3))) % 2)
        y1 = y + flips[0] * (1 - 2 * (y % 2))
        y2 = y1 + flips[1] * (3 - 2 * y1)
        z1 = z + flips[2] * (1 - 2 * (z % 2))
        z2 = z1 + flips[3] * (3 - 2 * z1)
        row = pl.multiple_of((z2 * 4 + y2) * 64 + k * 16, 16)
        place = pl.multiple_of(half * 512 + k * 128 + (position % 8) * 16, 16)
        pltpu.make_async_copy(og.at[pl.ds(row, 16)], g_v.at[pl.ds(place, 16)], load_sem.at[1]).start()
        pltpu.make_async_copy(act.at[pl.ds(row, 16)], a_v.at[pl.ds(place, 16)], load_sem.at[0]).start()
        return carry

    lax.fori_loop(0, 64, load, 0)

    barrier = pltpu.get_barrier_semaphore()
    for device in (sibling, near_a, near_b) + partners:
        pl.semaphore_signal(barrier, inc=1, device_id=device, device_id_type=MESH)
    pl.semaphore_wait(barrier, 7)

    def query_copy(a, h, j):
        src, dst = ((qi, qi_v), (qo, qo_v))[a]
        to = (sibling, near_a, near_b, sibling, sibling, near_b, near_a, sibling)[j]
        if j < 3:
            source = src.at[pl.ds(h * 128, 128)]
            target = dst.at[(h, NEAR_A[h], NEAR_B[h])[j], core]
        elif j in (3, 4, 7):
            source = target = dst.at[{3: NEAR_A, 4: NEAR_B, 7: FAR}[j][h], core]
        else:
            half = pl.ds((j - 5) * 64, 64)
            source = dst.at[(NEAR_A, NEAR_B)[j - 5][h], core, half]
            target = dst.at[FAR[h], core, half]
        return pltpu.make_async_remote_copy(
            source, target, q_send.at[a, h, j], q_recv.at[a, h, j], device_id=to, device_id_type=MESH
        )

    def start_queries(h, js):
        for j in js:
            for a in range(2):
                query_copy(a, h, j).start()

    def await_queries(h, j):
        for a in range(2):
            query_copy(a, h, j).wait_recv()

    start_queries(0, (0, 1, 2))
    start_queries(1, (0,))

    def message(step, level, k):
        return pltpu.make_async_remote_copy(
            sends[level].at[step, k], recvs[level].at[step, k], m_send.at[step, level, k], m_recv.at[step, level, k],
            device_id=partners[(k + level) % 4], device_id_type=MESH,
        )

    def arrivals(step):
        for h in range(2):
            @pl.when(step == h)
            def _():
                own[2 * h].wait()
                own[2 * h + 1].wait()
                await_queries(h, 0)

            @pl.when(step == NEAR_A[h])
            def _():
                await_queries(h, 1)
                start_queries(h, (5, 3))
                await_queries(h, 2)
                start_queries(h, (6, 4))
                if h == 0:
                    start_queries(1, (1, 2))
                await_queries(h, 3)

            @pl.when(step == NEAR_B[h])
            def _():
                await_queries(h, 4)

            @pl.when(step == FAR[h])
            def _():
                await_queries(h, 5)
                await_queries(h, 6)
                start_queries(h, (7,))
                await_queries(h, 7)

        @pl.when(step == 0)
        def _():
            pltpu.make_async_copy(og, g_v, load_sem.at[1]).wait()
            pltpu.make_async_copy(act, a_v, load_sem.at[0]).wait()

    def multiply(step):
        slot = step % SLOTS
        for t, (tokens, queries) in enumerate(((a_v, qi_v), (g_v, qo_v))):
            weights = queries[step].reshape(256, queries.shape[3])
            for m in range(2):
                block = lax.dot_general(
                    tokens[pl.ds(m * 512, 512), :], weights, (((1,), (1,)), ((), ())), preferred_element_type=F32
                )
                part[slot, 2 * t, pl.ds(m * 512, 512), :] = block[:, :128]
                part[slot, 2 * t + 1, pl.ds(m * 512, 512), :] = block[:, 128:]
        inverse, top_bounds = [], []
        for t in range(2):
            top = jnp.max(jnp.abs(part[slot, pl.ds(2 * t, 2)].reshape(256, 8, 128)), axis=0)
            top = jnp.max(jnp.max(top, axis=1, keepdims=True), axis=0, keepdims=True)
            bound = bound_above(jnp.broadcast_to(top, (8, 128)))
            for k in range(STREAMS):
                bounds[slot, k, t] = bound
            top_bounds.append(bound)
            inverse.append(TOP / bound)
        for k in range(STREAMS):
            s1[step, k, pl.ds(512, 16), :] = jnp.concatenate(top_bounds, axis=0).astype(BF16)
            for ct in range(4):
                value = tiles(part[slot, ct, pl.ds(512 + k * 128, 128), :])
                s1[step, k, pl.ds(ct * 128, 128), :] = rows_of(encode(value, inverse[ct // 2]))
            message(step, 0, k).start()

    def received(step, level, k, ct, first, count, scale):
        n = 128 >> level
        slot = step % SLOTS
        value = tiles(part[slot, ct, pl.ds(k * 128 + first, count), :])
        return value + decode(tiles(recvs[level][step, k, pl.ds(ct * n + first, count), :]), scale)

    def pass_on(step, level):
        n = 128 >> level
        m = n // 2
        slot = step % SLOTS
        scales = []
        for k in range(STREAMS):
            message(step, level, k).wait()
            theirs = recvs[level][step, k, pl.ds(4 * n, 16), :].astype(F32)
            scale, inverse, fresh = [], [], []
            for t in range(2):
                their = theirs[8 * t : 8 * t + 8]
                bound = bound_above(bounds[slot, k, t] + their)
                bounds[slot, k, t] = bound
                fresh.append(bound)
                scale.append(their * (1.0 / TOP))
                inverse.append(TOP / bound)
            sends[level + 1][step, k, pl.ds(4 * m, 16), :] = jnp.concatenate(fresh, axis=0).astype(BF16)
            for ct in range(4):
                total = received(step, level, k, ct, m, m, scale[ct // 2])
                sends[level + 1][step, k, pl.ds(ct * m, m), :] = rows_of(encode(total, inverse[ct // 2]))
            message(step, level + 1, k).start()
            scales.append(scale)
        for k in range(STREAMS):
            for ct in range(4):
                total = received(step, level, k, ct, 0, m, scales[k][ct // 2])
                part[slot, ct, pl.ds(k * 128, m), :] = rows_of(total)

    def finish(step):
        last = LEVELS - 1
        for k in range(STREAMS):
            message(step, last, k).wait()
            theirs = recvs[last][step, k, pl.ds(64, 16), :].astype(F32)
            scale = [theirs[:8] * (1.0 / TOP), theirs[8:] * (1.0 / TOP)]
            total = [rows_of(received(step, last, k, ct, 0, 16, scale[ct // 2])) for ct in range(4)]
            for c in range(2):
                prod[pl.ds(k * 16, 16), pl.ds(c * 128, 128)] = total[c] * total[2 + c]
        place = (step - 2) % 3
        half = jnp.where(step < 2, step, (step - 2) // 3)
        chip = jnp.where(place == 0, flip_one(x), jnp.where(place == 1, flip_three(x), (x + 2) % 4))
        chip = jnp.where(step < 2, x, chip)
        row = lax.broadcasted_iota(jnp.int32, (256, 64), 0)
        column = lax.broadcasted_iota(jnp.int32, (256, 64), 1)
        query = chip * 16 + (row // 128) * 8 + half * 4 + (row % 128) // RANK
        pick = jnp.where(query == column, 1.0, 0.0).astype(F32)
        sums = jnp.dot(prod[...], pick, precision=lax.Precision.HIGHEST, preferred_element_type=F32)
        out[...] += sums * RANK**-0.5

    out[...] = jnp.zeros_like(out)

    def of_turn(turn):
        step = turn
        fits = turn >= 0
        for idle in reversed(IDLE):
            step = jnp.where(turn > idle, step - 1, step)
            fits = jnp.logical_and(fits, turn != idle)
        return step, jnp.logical_and(fits, step < STEPS)

    def turn_body(turn, carry):
        step, fits = of_turn(turn)

        @pl.when(fits)
        def _():
            arrivals(step)
            multiply(step)

        for level in range(LEVELS - 1):
            step_l, fits_l = of_turn(turn - 1 - level)

            @pl.when(fits_l)
            def _():
                pass_on(step_l, level)

        step_f, fits_f = of_turn(turn - LEVELS)

        @pl.when(fits_f)
        def _():
            finish(step_f)

        return carry

    lax.fori_loop(0, TURNS, turn_body, 0)

    for h in range(2):
        for j in range(8):
            for a in range(2):
                query_copy(a, h, j).wait_send()


def shards(activations, out_grads, query_out, query_in):
    ff, d = activations.shape[1], out_grads.shape[1]
    rows = [4 * (128 >> level) + 16 for level in range(LEVELS)]
    messages = [pltpu.VMEM((STEPS, STREAMS, r, 128), BF16) for r in rows]
    return pl.pallas_call(
        kernel,
        out_shape=jax.ShapeDtypeStruct((64, 64), F32),
        in_specs=[pl.BlockSpec(memory_space=pl.ANY)] * 4,
        out_specs=pl.BlockSpec(memory_space=pltpu.VMEM),
        scratch_shapes=[
            pltpu.VMEM((1024, ff), BF16),
            pltpu.VMEM((1024, d), BF16),
            pltpu.VMEM((STEPS, 2, 128, ff), BF16),
            pltpu.VMEM((STEPS, 2, 128, d), BF16),
            pltpu.VMEM((SLOTS, 4, 1024, 128), F32),
            pltpu.VMEM((SLOTS, STREAMS, 2, 8, 128), F32),
            pltpu.VMEM((64, 256), F32),
            *messages,
            *messages,
            pltpu.SemaphoreType.DMA((2,)),
            pltpu.SemaphoreType.DMA((2, 2)),
            pltpu.SemaphoreType.DMA((2, 2, 8)),
            pltpu.SemaphoreType.DMA((2, 2, 8)),
            pltpu.SemaphoreType.DMA((STEPS, LEVELS, STREAMS)),
            pltpu.SemaphoreType.DMA((STEPS, LEVELS, STREAMS)),
        ],
        compiler_params=pltpu.CompilerParams(
            collective_id=0, has_side_effects=True, vmem_limit_bytes=56 * 1024 * 1024
        ),
    )(
        activations,
        out_grads,
        query_in.reshape(256, ff),
        query_out.reshape(256, d),
    )


def solution(mesh):
    return jax.shard_map(
        shards,
        mesh=mesh,
        in_specs=(
            P("tok", "feat"),
            P("tok", "feat"),
            P("tok", None, "feat"),
            P("tok", None, "feat"),
        ),
        out_specs=P(("tok", "feat"), None),
        check_vma=False,
    )
```

time: 1270 us -> 86.9 us (0.07)
  waiting for transfers between devices: 1200 us -> 0 us
  Pallas kernels: 0 us -> 85.3 us
  matrix products: 45.5 us -> 0 us
  between operations: 13.1 us -> 0.01 us
    reduce_scatter x16 -> x0, waiting for transfers between devices: 1050 us -> none  [the longest x8 604 us: block_scores(): lax.psum_scatter(act_proj, 'feat', scatter_dimension=0, tiled=True)]
    ppermute x14 -> x0, waiting for transfers between devices: 147 us -> none  [passed_along(): return lax.ppermute(value, axis, pairs)]
    pallas_call x0 -> x1, Pallas kernels: none -> 85.3 us  [shards(): pl.pallas_call(kernel, out_shape=jax.ShapeDtypeStruct((64, 64), F32), in_...]
    dot_general x16 -> x0, matrix products: 45.5 us -> none  [the longest x8 33.8 us: project(): jnp.einsum('tf,cf->tc', activations, flat_inner, preferred_element_type=j...]
  transfers between devices with their start and end apart: 30 -> 0, of which waited for: 30 -> 0; matrix products, arithmetic and copies ran while one was open for 2% -> 0% of each run, Pallas kernels for 0% -> 0%
where the time goes in v1:
time: 86.9 us; the launch traced here: 86.7 us
  Pallas kernels  85.3 us (98%)
  local copies, waits for them, and re-layouts  1.38 us (2%)
    pallas_call x1, Pallas kernels, shards(): pl.pallas_call(kernel, out_shape=jax.ShapeDtypeStruct((64, 64), F32), in_...  85.3 us

profile of v1, /device:TPU:0, one launch (start us, length us, event | category | flops | bytes accessed | tf_op | source)
XLA Modules:
  0.0 86.7 jit_solution(1884684362544261336)
XLA Ops:
  0.0 85.3 %shard_map.46 = f32[64,64]{1,0:T(8,128)} custom-call(bf16[1024,1792]{1,0:T(8,128)(2,1)} %act.1, bf16[1024,512]{1,0:T(8,128)(2,1)} %og.1, bf16[256,1792]{1,0:T(8,128)(2,1)} %bitcast.2, bf16[256,512]{1,0:T(8,128)(2,1)} %bitcast.3), custom_call_target="tpu_custom_call" | custom-call | tf_op jit(solution)/shard_map/pallas_call | solution.py:305
  85.3 1.4 %copy.6 = f32[64,64]{1,0:T(8,128)} copy(f32[64,64]{1,0:T(8,128)} %shard_map.46) | data formatting | bytes 32768

commit v2 on v1

v2 whole, which is shorter than its diff:
```python
import jax
import jax.numpy as jnp
from jax import lax
from jax.experimental import pallas as pl
from jax.experimental.pallas import tpu as pltpu
from jax.sharding import PartitionSpec as P

RANK = 32
MESH = pl.DeviceIdType.MESH
F32 = jnp.float32
BF16 = jnp.bfloat16

STREAMS = 4
LEVELS = 4
STEPS = 8
LAGS = (1, 2, 3, 4)
SLOTS = 8
POWER = 17
TOP = 2.0 ** (127.0 / POWER)
TINY = 2.0**-100
IDLE = (2,)
TURNS = STEPS + len(IDLE) + LAGS[-1]


def order_of(k):
    return [(k + level) % 4 for level in range(LEVELS)]


def bit(group, d):
    return (group >> (3 - d)) % 2


def kept(k, level):
    return [g for g in range(16) if not any(bit(g, d) for d in order_of(k)[: level + 1])]


def split(k, level):
    held = range(16) if level == 0 else kept(k, level - 1)
    d = order_of(k)[level]
    return [g for g in held if bit(g, d)], [g for g in held if not bit(g, d)]


def rows_at(group, k):
    return pl.ds(group * 64 + k * 16, 16)


def flip_one(v):
    return v + 1 - 2 * (v % 2)


def flip_three(v):
    return 3 - v


def encode(value, inverse):
    n = value * inverse
    n2 = n * n
    n4 = n2 * n2
    n8 = n4 * n4
    return (n8 * n8 * n).astype(BF16)


def decode(sent, scale):
    y = sent.astype(F32)
    log = jnp.log2(jnp.maximum(jnp.abs(y), 2.0**-126))
    return y * jnp.exp2(log * (1.0 / POWER - 1.0)) * scale


def bound_above(bound):
    return jnp.maximum((bound * 1.01).astype(BF16).astype(F32), TINY)


def tiles(value):
    return value.reshape(value.shape[0] // 8, 8, 128)


def rows_of(value):
    return value.reshape(value.shape[0] * 8, 128)


def kernel(
    act, og, qi, qo, out,
    a_v, g_v, qi_v, qo_v, part, bounds, prod,
    s1, s2, s3, s4, r1, r2, r3, r4,
    load_sem, own_sem, sib_send, sib_recv, near_send, near_recv, pass_send, pass_recv,
    relay_send, relay_recv, far_send, far_recv, m_send, m_recv,
):
    tok = lax.axis_index("tok")
    feat = lax.axis_index("feat")
    x, core = tok // 2, tok % 2
    z, y = feat // 4, feat % 4
    sibling = (tok + 1 - 2 * core, feat)
    near_a = (flip_one(x) * 2 + core, feat)
    near_b = (flip_three(x) * 2 + core, feat)
    partners = (
        (tok, z * 4 + flip_one(y)),
        (tok, z * 4 + flip_three(y)),
        (tok, flip_one(z) * 4 + y),
        (tok, flip_three(z) * 4 + y),
    )
    sends, recvs = (s1, s2, s3, s4), (r1, r2, r3, r4)

    barrier = pltpu.get_barrier_semaphore()
    for device in (sibling, near_a, near_b) + partners:
        pl.semaphore_signal(barrier, inc=1, device_id=device, device_id_type=MESH)

    arrays = ((qi, qi_v), (qo, qo_v))

    def own_copy(h, a):
        src, dst = arrays[a]
        return pltpu.make_async_copy(src.at[pl.ds(2 * h, 2)], dst.at[h, pl.ds(2 * core, 2)], own_sem.at[h, a])

    for h in range(2):
        for a in range(2):
            own_copy(h, a).start()
    for group in range(16):
        gy = flip_one(y) if bit(group, 0) else y
        gy = flip_three(gy) if bit(group, 1) else gy
        gz = flip_one(z) if bit(group, 2) else z
        gz = flip_three(gz) if bit(group, 3) else gz
        row = pl.multiple_of((gz * 4 + gy) * 64, 64)
        pltpu.make_async_copy(og.at[pl.ds(row, 64)], g_v.at[pl.ds(group * 64, 64)], load_sem.at[1]).start()
        pltpu.make_async_copy(act.at[pl.ds(row, 64)], a_v.at[pl.ds(group * 64, 64)], load_sem.at[0]).start()

    def remote(src, dst, send, recv, device):
        return pltpu.make_async_remote_copy(src, dst, send, recv, device_id=device, device_id_type=MESH)

    def sibling_copy(h, a):
        src, dst = arrays[a]
        return remote(src.at[pl.ds(2 * h, 2)], dst.at[h, pl.ds(2 * core, 2)], sib_send.at[h, a], sib_recv.at[h, a], sibling)

    def near_copy(q, a, side):
        src, dst = arrays[a]
        return remote(
            src.at[q], dst.at[2 + q, 2 * side + core], near_send.at[q, a, side], near_recv.at[q, a, side], (near_a, near_b)[side]
        )

    def pass_copy(q, a, side):
        place = arrays[a][1].at[2 + q, 2 * side + core]
        return remote(place, place, pass_send.at[q, a, side], pass_recv.at[q, a, side], sibling)

    def relay_copy(q, a, side):
        dst, half = arrays[a][1], pl.ds(32 * side, 32)
        return remote(
            dst.at[2 + q, 2 * side + core, half], dst.at[6 + q // 2, 2 * core + q % 2, half],
            relay_send.at[q, a, side], relay_recv.at[q, a, side], (near_b, near_a)[side],
        )

    def far_copy(h, a):
        place = arrays[a][1].at[6 + h, pl.ds(2 * core, 2)]
        return remote(place, place, far_send.at[h, a], far_recv.at[h, a], sibling)

    pl.semaphore_wait(barrier, 7)
    for q in range(4):
        for side in range(2):
            for a in range(2):
                near_copy(q, a, side).start()
        if q < 2:
            for a in range(2):
                sibling_copy(q, a).start()

    def message(step, level, k):
        return remote(
            sends[level].at[step, k], recvs[level].at[step, k], m_send.at[step, level, k], m_recv.at[step, level, k],
            partners[order_of(k)[level]],
        )

    def hand_over(step):
        for q in range(4):
            @pl.when(step == 2 + q)
            def _():
                for side in range(2):
                    for a in range(2):
                        near_copy(q, a, side).wait_recv()
                        relay_copy(q, a, side).start()
                        pass_copy(q, a, side).start()

        for h in range(2):
            @pl.when(step == 6 + h)
            def _():
                for a in range(2):
                    for q in (2 * h, 2 * h + 1):
                        for side in range(2):
                            relay_copy(q, a, side).wait_recv()
                    far_copy(h, a).start()

    def arrivals(step):
        for h in range(2):
            @pl.when(step == h)
            def _():
                for a in range(2):
                    own_copy(h, a).wait()
                    sibling_copy(h, a).wait_recv()

        for q in range(4):
            @pl.when(step == 2 + q)
            def _():
                for side in range(2):
                    for a in range(2):
                        pass_copy(q, a, side).wait_recv()

        for h in range(2):
            @pl.when(step == 6 + h)
            def _():
                for a in range(2):
                    far_copy(h, a).wait_recv()

        @pl.when(step == 0)
        def _():
            pltpu.make_async_copy(og, g_v, load_sem.at[1]).wait()
            pltpu.make_async_copy(act, a_v, load_sem.at[0]).wait()

    def multiply(step):
        slot = step % SLOTS
        for t, (tokens, queries) in enumerate(((a_v, qi_v), (g_v, qo_v))):
            weights = queries[step].reshape(256, queries.shape[3])
            for m in range(2):
                block = lax.dot_general(
                    tokens[pl.ds(m * 512, 512), :], weights, (((1,), (1,)), ((), ())), preferred_element_type=F32
                )
                part[slot, 2 * t, pl.ds(m * 512, 512), :] = block[:, :128]
                part[slot, 2 * t + 1, pl.ds(m * 512, 512), :] = block[:, 128:]
        inverse, top_bounds = [], []
        for t in range(2):
            top = jnp.max(jnp.abs(part[slot, pl.ds(2 * t, 2)].reshape(256, 8, 128)), axis=0)
            top = jnp.max(jnp.max(top, axis=1, keepdims=True), axis=0, keepdims=True)
            bound = bound_above(jnp.broadcast_to(top, (8, 128)))
            for k in range(STREAMS):
                bounds[slot, k, t] = bound
            top_bounds.append(bound)
            inverse.append(TOP / bound)
        for k in range(STREAMS):
            s1[step, k, pl.ds(512, 16), :] = jnp.concatenate(top_bounds, axis=0).astype(BF16)
            for ct in range(4):
                for i, group in enumerate(split(k, 0)[0]):
                    value = tiles(part[slot, ct, rows_at(group, k), :])
                    s1[step, k, pl.ds(ct * 128 + i * 16, 16), :] = rows_of(encode(value, inverse[ct // 2]))
            message(step, 0, k).start()

    def total_of(step, level, k, ct, group, scale):
        n = 128 >> level
        value = tiles(part[step % SLOTS, ct, rows_at(group, k), :])
        place = pl.ds(ct * n + kept(k, level).index(group) * 16, 16)
        return value + decode(tiles(recvs[level][step, k, place, :]), scale)

    def pass_on(step, level):
        n = 128 >> level
        m = n // 2
        slot = step % SLOTS
        scales = []
        for k in range(STREAMS):
            message(step, level, k).wait()
            theirs = recvs[level][step, k, pl.ds(4 * n, 16), :].astype(F32)
            scale, inverse, fresh = [], [], []
            for t in range(2):
                their = theirs[8 * t : 8 * t + 8]
                bound = bound_above(bounds[slot, k, t] + their)
                bounds[slot, k, t] = bound
                fresh.append(bound)
                scale.append(their * (1.0 / TOP))
                inverse.append(TOP / bound)
            sends[level + 1][step, k, pl.ds(4 * m, 16), :] = jnp.concatenate(fresh, axis=0).astype(BF16)
            for ct in range(4):
                for i, group in enumerate(split(k, level + 1)[0]):
                    total = total_of(step, level, k, ct, group, scale[ct // 2])
                    sends[level + 1][step, k, pl.ds(ct * m + i * 16, 16), :] = rows_of(encode(total, inverse[ct // 2]))
            message(step, level + 1, k).start()
            scales.append(scale)
        for k in range(STREAMS):
            for ct in range(4):
                for group in split(k, level + 1)[1]:
                    total = total_of(step, level, k, ct, group, scales[k][ct // 2])
                    part[slot, ct, rows_at(group, k), :] = rows_of(total)

    def finish(step):
        last = LEVELS - 1
        for k in range(STREAMS):
            message(step, last, k).wait()
            theirs = recvs[last][step, k, pl.ds(64, 16), :].astype(F32)
            scale = [theirs[:8] * (1.0 / TOP), theirs[8:] * (1.0 / TOP)]
            total = [rows_of(total_of(step, last, k, ct, 0, scale[ct // 2])) for ct in range(4)]
            for c in range(2):
                prod[pl.ds(k * 16, 16), pl.ds(c * 128, 128)] = total[c] * total[2 + c]
        row = lax.broadcasted_iota(jnp.int32, (256, 64), 0)
        column = lax.broadcasted_iota(jnp.int32, (256, 64), 1)
        block = row // 64
        near = jnp.logical_and(step >= 2, step < 6)
        chip = jnp.where(step < 2, x, (x + 2) % 4)
        chip = jnp.where(near, jnp.where(block < 2, flip_one(x), flip_three(x)), chip)
        side = jnp.where(near, block % 2, block // 2)
        quarter = jnp.where(near, step - 2, 2 * (step % 2) + block % 2)
        query = chip * 16 + side * 8 + quarter * 2 + (row % 64) // RANK
        pick = jnp.where(query == column, 1.0, 0.0).astype(F32)
        sums = jnp.dot(prod[...], pick, precision=lax.Precision.HIGHEST, preferred_element_type=F32)
        out[...] += sums * RANK**-0.5

    out[...] = jnp.zeros_like(out)

    def of_turn(turn):
        step = turn
        fits = turn >= 0
        for idle in reversed(IDLE):
            step = jnp.where(turn > idle, step - 1, step)
            fits = jnp.logical_and(fits, turn != idle)
        return step, jnp.logical_and(fits, step < STEPS)

    def turn_body(turn, carry):
        step, fits = of_turn(turn)

        @pl.when(fits)
        def _():
            arrivals(step)
            multiply(step)

        for level in range(LEVELS - 1):
            step_l, fits_l = of_turn(turn - LAGS[level])

            @pl.when(fits_l)
            def _():
                pass_on(step_l, level)

        step_f, fits_f = of_turn(turn - LAGS[-1])

        @pl.when(fits_f)
        def _():
            finish(step_f)

        step_n, fits_n = of_turn(turn + 1)

        @pl.when(fits_n)
        def _():
            hand_over(step_n)

        return carry

    lax.fori_loop(0, TURNS, turn_body, 0)

    for a in range(2):
        for h in range(2):
            sibling_copy(h, a).wait_send()
            far_copy(h, a).wait_send()
        for q in range(4):
            for side in range(2):
                near_copy(q, a, side).wait_send()
                pass_copy(q, a, side).wait_send()
                relay_copy(q, a, side).wait_send()


def shards(activations, out_grads, query_out, query_in):
    ff, d = activations.shape[1], out_grads.shape[1]
    rows = [4 * (128 >> level) + 16 for level in range(LEVELS)]
    messages = [pltpu.VMEM((STEPS, STREAMS, r, 128), BF16) for r in rows]
    return pl.pallas_call(
        kernel,
        out_shape=jax.ShapeDtypeStruct((64, 64), F32),
        in_specs=[pl.BlockSpec(memory_space=pl.ANY)] * 4,
        out_specs=pl.BlockSpec(memory_space=pltpu.VMEM),
        scratch_shapes=[
            pltpu.VMEM((1024, ff), BF16),
            pltpu.VMEM((1024, d), BF16),
            pltpu.VMEM((STEPS, 4, 64, ff), BF16),
            pltpu.VMEM((STEPS, 4, 64, d), BF16),
            pltpu.VMEM((SLOTS, 4, 1024, 128), F32),
            pltpu.VMEM((SLOTS, STREAMS, 2, 8, 128), F32),
            pltpu.VMEM((64, 256), F32),
            *messages,
            *messages,
            pltpu.SemaphoreType.DMA((2,)),
            pltpu.SemaphoreType.DMA((2, 2)),
            *[pltpu.SemaphoreType.DMA((2, 2))] * 2,
            *[pltpu.SemaphoreType.DMA((4, 2, 2))] * 6,
            *[pltpu.SemaphoreType.DMA((2, 2))] * 2,
            pltpu.SemaphoreType.DMA((STEPS, LEVELS, STREAMS)),
            pltpu.SemaphoreType.DMA((STEPS, LEVELS, STREAMS)),
        ],
        compiler_params=pltpu.CompilerParams(
            collective_id=0, has_side_effects=True, vmem_limit_bytes=56 * 1024 * 1024
        ),
    )(
        activations,
        out_grads,
        query_in.reshape(4, 64, ff),
        query_out.reshape(4, 64, d),
    )


def solution(mesh):
    return jax.shard_map(
        shards,
        mesh=mesh,
        in_specs=(
            P("tok", "feat"),
            P("tok", "feat"),
            P("tok", None, "feat"),
            P("tok", None, "feat"),
        ),
        out_specs=P(("tok", "feat"), None),
        check_vma=False,
    )
```

time: 86.9 us -> 74.9 us (0.86)
  Pallas kernels: 85.3 us -> 73.4 us
    pallas_call x1, Pallas kernels: 85.3 us -> 73.4 us  [shards(): pl.pallas_call(kernel, out_shape=jax.ShapeDtypeStruct((64, 64), F32), in_...]
where the time goes in v2:
time: 74.9 us; the launch traced here: 74.8 us
  Pallas kernels  73.4 us (98%)
  local copies, waits for them, and re-layouts  1.38 us (2%)
    pallas_call x1, Pallas kernels, shards(): pl.pallas_call(kernel, out_shape=jax.ShapeDtypeStruct((64, 64), F32), in_...  73.4 us

profile of v2, /device:TPU:0, one launch (start us, length us, event | category | flops | bytes accessed | tf_op | source)
XLA Modules:
  0.0 74.8 jit_solution(10617173899520458072)
XLA Ops:
  0.0 73.4 %shard_map.46 = f32[64,64]{1,0:T(8,128)} custom-call(bf16[1024,1792]{1,0:T(8,128)(2,1)} %act.1, bf16[1024,512]{1,0:T(8,128)(2,1)} %og.1, bf16[4,64,1792]{2,1,0:T(8,128)(2,1)} %bitcast.2, bf16[4,64,512]{2,1,0:T(8,128)(2,1)} %bitcast.3), custom_call_target="tpu_custom_call" | custom-call | tf_op jit(solution)/shard_map/pallas_call | solution.py:353
  73.4 1.4 %copy.6 = f32[64,64]{1,0:T(8,128)} copy(f32[64,64]{1,0:T(8,128)} %shard_map.46) | data formatting | bytes 32768

commit v3 on v2

--- a/solution.py
+++ b/solution.py
@@ -15,11 +15,13 @@
 STEPS = 8
 LAGS = (1, 2, 3, 4)
 SLOTS = 8
+DIRECT = 7
 POWER = 17
 TOP = 2.0 ** (127.0 / POWER)
 TINY = 2.0**-100
-IDLE = (2,)
-TURNS = STEPS + len(IDLE) + LAGS[-1]
+IDLE = ()
+AHEAD = 1
+TURNS = STEPS + len(IDLE) + LAGS[-2]
 
 
 def order_of(k):
@@ -38,6 +40,11 @@
     held = range(16) if level == 0 else kept(k, level - 1)
     d = order_of(k)[level]
     return [g for g in held if bit(g, d)], [g for g in held if not bit(g, d)]
+
+
+def last_groups(k):
+    third, fourth = order_of(k)[2:]
+    return [8 >> third, 8 >> fourth, (8 >> third) + (8 >> fourth)]
 
 
 def rows_at(group, k):
@@ -81,9 +88,9 @@
 def kernel(
     act, og, qi, qo, out,
     a_v, g_v, qi_v, qo_v, part, bounds, prod,
-    s1, s2, s3, s4, r1, r2, r3, r4,
+    s1, s2, s3, s4, r1, r2, r3, r4, ds, dr,
     load_sem, own_sem, sib_send, sib_recv, near_send, near_recv, pass_send, pass_recv,
-    relay_send, relay_recv, far_send, far_recv, m_send, m_recv,
+    relay_send, relay_recv, far_send, far_recv, m_send, m_recv, d_send, d_recv,
 ):
     tok = lax.axis_index("tok")
     feat = lax.axis_index("feat")
@@ -100,8 +107,17 @@
     )
     sends, recvs = (s1, s2, s3, s4), (r1, r2, r3, r4)
 
+    def device_of(group):
+        gy = flip_one(y) if bit(group, 0) else y
+        gy = flip_three(gy) if bit(group, 1) else gy
+        gz = flip_one(z) if bit(group, 2) else z
+        gz = flip_three(gz) if bit(group, 3) else gz
+        return gz * 4 + gy
+
+    corners = tuple((tok, device_of(last_groups(k)[2])) for k in range(STREAMS))
+
     barrier = pltpu.get_barrier_semaphore()
-    for device in (sibling, near_a, near_b) + partners:
+    for device in (sibling, near_a, near_b) + partners + corners:
         pl.semaphore_signal(barrier, inc=1, device_id=device, device_id_type=MESH)
 
     arrays = ((qi, qi_v), (qo, qo_v))
@@ -114,11 +130,7 @@
         for a in range(2):
             own_copy(h, a).start()
     for group in range(16):
-        gy = flip_one(y) if bit(group, 0) else y
-        gy = flip_three(gy) if bit(group, 1) else gy
-        gz = flip_one(z) if bit(group, 2) else z
-        gz = flip_three(gz) if bit(group, 3) else gz
-        row = pl.multiple_of((gz * 4 + gy) * 64, 64)
+        row = pl.multiple_of(device_of(group) * 64, 64)
         pltpu.make_async_copy(og.at[pl.ds(row, 64)], g_v.at[pl.ds(group * 64, 64)], load_sem.at[1]).start()
         pltpu.make_async_copy(act.at[pl.ds(row, 64)], a_v.at[pl.ds(group * 64, 64)], load_sem.at[0]).start()
 
@@ -146,11 +158,11 @@
             relay_send.at[q, a, side], relay_recv.at[q, a, side], (near_b, near_a)[side],
         )
 
-    def far_copy(h, a):
-        place = arrays[a][1].at[6 + h, pl.ds(2 * core, 2)]
-        return remote(place, place, far_send.at[h, a], far_recv.at[h, a], sibling)
-
-    pl.semaphore_wait(barrier, 7)
+    def far_copy(q, a):
+        place = arrays[a][1].at[6 + q // 2, 2 * core + q % 2]
+        return remote(place, place, far_send.at[q, a], far_recv.at[q, a], sibling)
+
+    pl.semaphore_wait(barrier, 11)
     for q in range(4):
         for side in range(2):
             for a in range(2):
@@ -165,7 +177,13 @@
             partners[order_of(k)[level]],
         )
 
-    def hand_over(step):
+    def direct(step, k, j):
+        return remote(
+            ds.at[step - DIRECT, k, j], dr.at[step - DIRECT, k, j], d_send.at[step - DIRECT, k, j], d_recv.at[step - DIRECT, k, j],
+            (tok, device_of(last_groups(k)[j])),
+        )
+
+    def hand_over_near(step):
         for q in range(4):
             @pl.when(step == 2 + q)
             def _():
@@ -175,14 +193,15 @@
                         relay_copy(q, a, side).start()
                         pass_copy(q, a, side).start()
 
+    def hand_over_far(step):
         for h in range(2):
             @pl.when(step == 6 + h)
             def _():
-                for a in range(2):
-                    for q in (2 * h, 2 * h + 1):
+                for q in (2 * h, 2 * h + 1):
+                    for a in range(2):
                         for side in range(2):
                             relay_copy(q, a, side).wait_recv()
-                    far_copy(h, a).start()
+                        far_copy(q, a).start()
 
     def arrivals(step):
         for h in range(2):
@@ -203,7 +222,8 @@
             @pl.when(step == 6 + h)
             def _():
                 for a in range(2):
-                    far_copy(h, a).wait_recv()
+                    for q in (2 * h, 2 * h + 1):
+                        far_copy(q, a).wait_recv()
 
         @pl.when(step == 0)
         def _():
@@ -272,6 +292,35 @@
                     total = total_of(step, level, k, ct, group, scales[k][ct // 2])
                     part[slot, ct, rows_at(group, k), :] = rows_of(total)
 
+    def next_bounds(step, k, theirs):
+        scale, inverse, fresh = [], [], []
+        for t in range(2):
+            their = theirs[8 * t : 8 * t + 8]
+            bound = bound_above(bounds[step % SLOTS, k, t] + their)
+            fresh.append(bound)
+            scale.append(their * (1.0 / TOP))
+            inverse.append(TOP / bound)
+        return scale, inverse, jnp.concatenate(fresh, axis=0).astype(BF16)
+
+    def spread(step):
+        level, slot = 1, step % SLOTS
+        scales = []
+        for k in range(STREAMS):
+            message(step, level, k).wait()
+            theirs = recvs[level][step, k, pl.ds(4 * 64, 16), :].astype(F32)
+            scale, inverse, fresh = next_bounds(step, k, theirs)
+            for j, group in enumerate(last_groups(k)):
+                ds[step - DIRECT, k, j, pl.ds(64, 16), :] = fresh
+                for ct in range(4):
+                    total = total_of(step, level, k, ct, group, scale[ct // 2])
+                    ds[step - DIRECT, k, j, pl.ds(ct * 16, 16), :] = rows_of(encode(total, inverse[ct // 2]))
+                direct(step, k, j).start()
+            scales.append(scale)
+        for k in range(STREAMS):
+            for ct in range(4):
+                total = total_of(step, level, k, ct, 0, scales[k][ct // 2])
+                part[slot, ct, rows_at(0, k), :] = rows_of(total)
+
     def finish(step):
         last = LEVELS - 1
         for k in range(STREAMS):
@@ -281,6 +330,22 @@
             total = [rows_of(total_of(step, last, k, ct, 0, scale[ct // 2])) for ct in range(4)]
             for c in range(2):
                 prod[pl.ds(k * 16, 16), pl.ds(c * 128, 128)] = total[c] * total[2 + c]
+        add_scores(step)
+
+    def finish_direct(step):
+        for k in range(STREAMS):
+            total = [tiles(part[step % SLOTS, ct, rows_at(0, k), :]) for ct in range(4)]
+            for j in range(3):
+                direct(step, k, j).wait()
+                theirs = dr[step - DIRECT, k, j, pl.ds(64, 16), :].astype(F32)
+                scale = [theirs[:8] * (1.0 / TOP), theirs[8:] * (1.0 / TOP)]
+                for ct in range(4):
+                    total[ct] += decode(tiles(dr[step - DIRECT, k, j, pl.ds(ct * 16, 16), :]), scale[ct // 2])
+            for c in range(2):
+                prod[pl.ds(k * 16, 16), pl.ds(c * 128, 128)] = rows_of(total[c] * total[2 + c])
+        add_scores(step)
+
+    def add_scores(step):
         row = lax.broadcasted_iota(jnp.int32, (256, 64), 0)
         column = lax.broadcasted_iota(jnp.int32, (256, 64), 1)
         block = row // 64
@@ -312,24 +377,49 @@
             arrivals(step)
             multiply(step)
 
-        for level in range(LEVELS - 1):
-            step_l, fits_l = of_turn(turn - LAGS[level])
-
-            @pl.when(fits_l)
-            def _():
-                pass_on(step_l, level)
-
-        step_f, fits_f = of_turn(turn - LAGS[-1])
-
-        @pl.when(fits_f)
-        def _():
-            finish(step_f)
-
-        step_n, fits_n = of_turn(turn + 1)
+        step_0, fits_0 = of_turn(turn - LAGS[0])
+
+        @pl.when(fits_0)
+        def _():
+            pass_on(step_0, 0)
+
+        step_n, fits_n = of_turn(turn + AHEAD)
 
         @pl.when(fits_n)
         def _():
-            hand_over(step_n)
+            hand_over_near(step_n)
+
+        step_1, fits_1 = of_turn(turn - LAGS[1])
+
+        @pl.when(jnp.logical_and(fits_1, step_1 < DIRECT))
+        def _():
+            pass_on(step_1, 1)
+
+        @pl.when(jnp.logical_and(fits_1, step_1 >= DIRECT))
+        def _():
+            spread(step_1)
+
+        step_o, fits_o = of_turn(turn + 1)
+
+        @pl.when(fits_o)
+        def _():
+            hand_over_far(step_o)
+
+        step_2, fits_2 = of_turn(turn - LAGS[2])
+
+        @pl.when(jnp.logical_and(fits_2, step_2 < DIRECT))
+        def _():
+            pass_on(step_2, 2)
+
+        step_3, fits_3 = of_turn(turn - LAGS[3])
+
+        @pl.when(jnp.logical_and(fits_3, step_3 < DIRECT))
+        def _():
+            finish(step_3)
+
+        @pl.when(jnp.logical_and(fits_2, step_2 >= DIRECT))
+        def _():
+            finish_direct(step_2)
 
         return carry
 
@@ -338,8 +428,8 @@
     for a in range(2):
         for h in range(2):
             sibling_copy(h, a).wait_send()
-            far_copy(h, a).wait_send()
         for q in range(4):
+            far_copy(q, a).wait_send()
             for side in range(2):
                 near_copy(q, a, side).wait_send()
                 pass_copy(q, a, side).wait_send()
@@ -365,13 +455,14 @@
             pltpu.VMEM((64, 256), F32),
             *messages,
             *messages,
+            *[pltpu.VMEM((STEPS - DIRECT, STREAMS, 3, 80, 128), BF16)] * 2,
             pltpu.SemaphoreType.DMA((2,)),
             pltpu.SemaphoreType.DMA((2, 2)),
             *[pltpu.SemaphoreType.DMA((2, 2))] * 2,
             *[pltpu.SemaphoreType.DMA((4, 2, 2))] * 6,
-            *[pltpu.SemaphoreType.DMA((2, 2))] * 2,
-            pltpu.SemaphoreType.DMA((STEPS, LEVELS, STREAMS)),
-            pltpu.SemaphoreType.DMA((STEPS, LEVELS, STREAMS)),
+            *[pltpu.SemaphoreType.DMA((4, 2))] * 2,
+            *[pltpu.SemaphoreType.DMA((STEPS, LEVELS, STREAMS))] * 2,
+            *[pltpu.SemaphoreType.DMA((STEPS - DIRECT, STREAMS, 3))] * 2,
         ],
         compiler_params=pltpu.CompilerParams(
             collective_id=0, has_side_effects=True, vmem_limit_bytes=56 * 1024 * 1024

time: 74.9 us -> 71.9 us (0.960)
  Pallas kernels: 73.4 us -> 69.7 us
    pallas_call x1, Pallas kernels: 73.4 us -> 69.7 us  [shards(): pl.pallas_call(kernel, out_shape=jax.ShapeDtypeStruct((64, 64), F32), in_...]
where the time goes in v3:
time: 71.9 us; the launch traced here: 71.1 us
  Pallas kernels  69.7 us (97%)
  local copies, waits for them, and re-layouts  1.38 us (2%)
    pallas_call x1, Pallas kernels, shards(): pl.pallas_call(kernel, out_shape=jax.ShapeDtypeStruct((64, 64), F32), in_...  69.7 us

profile of v3, /device:TPU:0, one launch (start us, length us, event | category | flops | bytes accessed | tf_op | source)
XLA Modules:
  0.0 71.1 jit_solution(11045130274585998127)
XLA Ops:
  0.0 69.7 %shard_map.46 = f32[64,64]{1,0:T(8,128)} custom-call(bf16[1024,1792]{1,0:T(8,128)(2,1)} %act.1, bf16[1024,512]{1,0:T(8,128)(2,1)} %og.1, bf16[4,64,1792]{2,1,0:T(8,128)(2,1)} %bitcast.2, bf16[4,64,512]{2,1,0:T(8,128)(2,1)} %bitcast.3), custom_call_target="tpu_custom_call" | custom-call | tf_op jit(solution)/shard_map/pallas_call | solution.py:443
  69.7 1.4 %copy.6 = f32[64,64]{1,0:T(8,128)} copy(f32[64,64]{1,0:T(8,128)} %shard_map.46) | data formatting | bytes 32768

commit v4 on v3

--- a/solution.py
+++ b/solution.py
@@ -124,7 +124,7 @@
 
     def own_copy(h, a):
         src, dst = arrays[a]
-        return pltpu.make_async_copy(src.at[pl.ds(2 * h, 2)], dst.at[h, pl.ds(2 * core, 2)], own_sem.at[h, a])
+        return pltpu.make_async_copy(src.at[pl.ds(2 * h, 2)], dst.at[0, pl.ds(2 * h, 2)], own_sem.at[h, a])
 
     for h in range(2):
         for a in range(2):
@@ -139,7 +139,7 @@
 
     def sibling_copy(h, a):
         src, dst = arrays[a]
-        return remote(src.at[pl.ds(2 * h, 2)], dst.at[h, pl.ds(2 * core, 2)], sib_send.at[h, a], sib_recv.at[h, a], sibling)
+        return remote(src.at[pl.ds(2 * h, 2)], dst.at[1, pl.ds(2 * h, 2)], sib_send.at[h, a], sib_recv.at[h, a], sibling)
 
     def near_copy(q, a, side):
         src, dst = arrays[a]
@@ -204,11 +204,16 @@
                         far_copy(q, a).start()
 
     def arrivals(step):
-        for h in range(2):
-            @pl.when(step == h)
-            def _():
+        @pl.when(step == 0)
+        def _():
+            for h in range(2):
                 for a in range(2):
                     own_copy(h, a).wait()
+
+        @pl.when(step == 1)
+        def _():
+            for h in range(2):
+                for a in range(2):
                     sibling_copy(h, a).wait_recv()
 
         for q in range(4):
@@ -292,6 +297,24 @@
                     total = total_of(step, level, k, ct, group, scales[k][ct // 2])
                     part[slot, ct, rows_at(group, k), :] = rows_of(total)
 
+    def choice_of(step):
+        row = lax.broadcasted_iota(jnp.int32, (256, 64), 0)
+        column = lax.broadcasted_iota(jnp.int32, (256, 64), 1)
+        block = row // 64
+        near = jnp.logical_and(step >= 2, step < 6)
+        chip = jnp.where(step < 2, x, (x + 2) % 4)
+        chip = jnp.where(near, jnp.where(block < 2, flip_one(x), flip_three(x)), chip)
+        side = jnp.where(near, block % 2, block // 2)
+        side = jnp.where(step < 2, jnp.where(step == 0, core, 1 - core), side)
+        quarter = jnp.where(near, step - 2, 2 * (step % 2) + block % 2)
+        quarter = jnp.where(step < 2, block, quarter)
+        query = chip * 16 + side * 8 + quarter * 2 + (row % 64) // RANK
+        return jnp.where(query == column, 1.0, 0.0).astype(F32)
+
+    def add_scores(choice):
+        sums = jnp.dot(prod[...], choice, precision=lax.Precision.HIGHEST, preferred_element_type=F32)
+        out[...] += sums * RANK**-0.5
+
     def next_bounds(step, k, theirs):
         scale, inverse, fresh = [], [], []
         for t in range(2):
@@ -322,6 +345,7 @@
                 part[slot, ct, rows_at(0, k), :] = rows_of(total)
 
     def finish(step):
+        choice = choice_of(step)
         last = LEVELS - 1
         for k in range(STREAMS):
             message(step, last, k).wait()
@@ -330,9 +354,10 @@
             total = [rows_of(total_of(step, last, k, ct, 0, scale[ct // 2])) for ct in range(4)]
             for c in range(2):
                 prod[pl.ds(k * 16, 16), pl.ds(c * 128, 128)] = total[c] * total[2 + c]
-        add_scores(step)
+        add_scores(choice)
 
     def finish_direct(step):
+        choice = choice_of(step)
         for k in range(STREAMS):
             total = [tiles(part[step % SLOTS, ct, rows_at(0, k), :]) for ct in range(4)]
             for j in range(3):
@@ -343,23 +368,20 @@
                     total[ct] += decode(tiles(dr[step - DIRECT, k, j, pl.ds(ct * 16, 16), :]), scale[ct // 2])
             for c in range(2):
                 prod[pl.ds(k * 16, 16), pl.ds(c * 128, 128)] = rows_of(total[c] * total[2 + c])
-        add_scores(step)
-
-    def add_scores(step):
-        row = lax.broadcasted_iota(jnp.int32, (256, 64), 0)
-        column = lax.broadcasted_iota(jnp.int32, (256, 64), 1)
-        block = row // 64
-        near = jnp.logical_and(step >= 2, step < 6)
-        chip = jnp.where(step < 2, x, (x + 2) % 4)
-        chip = jnp.where(near, jnp.where(block < 2, flip_one(x), flip_three(x)), chip)
-        side = jnp.where(near, block % 2, block // 2)
-        quarter = jnp.where(near, step - 2, 2 * (step % 2) + block % 2)
-        query = chip * 16 + side * 8 + quarter * 2 + (row % 64) // RANK
-        pick = jnp.where(query == column, 1.0, 0.0).astype(F32)
-        sums = jnp.dot(prod[...], pick, precision=lax.Precision.HIGHEST, preferred_element_type=F32)
-        out[...] += sums * RANK**-0.5
+        add_scores(choice)
 
     out[...] = jnp.zeros_like(out)
+
+    def queries_sent():
+        for a in range(2):
+            for h in range(2):
+                sibling_copy(h, a).wait_send()
+            for q in range(4):
+                far_copy(q, a).wait_send()
+                for side in range(2):
+                    near_copy(q, a, side).wait_send()
+                    pass_copy(q, a, side).wait_send()
+                    relay_copy(q, a, side).wait_send()
 
     def of_turn(turn):
         step = turn
@@ -377,17 +399,27 @@
             arrivals(step)
             multiply(step)
 
+        @pl.when(turn == STEPS + len(IDLE))
+        def _():
+            queries_sent()
+
+        step_n, fits_n = of_turn(turn + AHEAD)
+
+        @pl.when(fits_n)
+        def _():
+            hand_over_near(step_n)
+
         step_0, fits_0 = of_turn(turn - LAGS[0])
 
         @pl.when(fits_0)
         def _():
             pass_on(step_0, 0)
 
-        step_n, fits_n = of_turn(turn + AHEAD)
-
-        @pl.when(fits_n)
-        def _():
-            hand_over_near(step_n)
+        step_o, fits_o = of_turn(turn + 1)
+
+        @pl.when(fits_o)
+        def _():
+            hand_over_far(step_o)
 
         step_1, fits_1 = of_turn(turn - LAGS[1])
 
@@ -399,12 +431,6 @@
         def _():
             spread(step_1)
 
-        step_o, fits_o = of_turn(turn + 1)
-
-        @pl.when(fits_o)
-        def _():
-            hand_over_far(step_o)
-
         step_2, fits_2 = of_turn(turn - LAGS[2])
 
         @pl.when(jnp.logical_and(fits_2, step_2 < DIRECT))
@@ -424,16 +450,6 @@
         return carry
 
     lax.fori_loop(0, TURNS, turn_body, 0)
-
-    for a in range(2):
-        for h in range(2):
-            sibling_copy(h, a).wait_send()
-        for q in range(4):
-            far_copy(q, a).wait_send()
-            for side in range(2):
-                near_copy(q, a, side).wait_send()
-                pass_copy(q, a, side).wait_send()
-                relay_copy(q, a, side).wait_send()
 
 
 def shards(activations, out_grads, query_out, query_in):
@@ -442,7 +458,7 @@
     messages = [pltpu.VMEM((STEPS, STREAMS, r, 128), BF16) for r in rows]
     return pl.pallas_call(
         kernel,
-        out_shape=jax.ShapeDtypeStruct((64, 64), F32),
+        out_shape=pltpu.VMEM((64, 64), F32),
         in_specs=[pl.BlockSpec(memory_space=pl.ANY)] * 4,
         out_specs=pl.BlockSpec(memory_space=pltpu.VMEM),
         scratch_shapes=[

time: 71.9 us -> 70.1 us (0.975)
  local copies, waits for them, and re-layouts: 1.38 us -> 0.62 us
    unnamed x1, local copies, waits for them, and re-layouts: 1.38 us -> 0.62 us
where the time goes in v4:
time: 70.1 us; the launch traced here: 70 us
  Pallas kernels  69.4 us (99%)
    pallas_call x1, Pallas kernels, shards(): pl.pallas_call(kernel, out_shape=pltpu.VMEM((64, 64), F32), in_specs=[pl....  69.4 us

profile of v4, /device:TPU:0, one launch (start us, length us, event | category | flops | bytes accessed | tf_op | source)
XLA Modules:
  0.0 70.0 jit_solution(1830856823661994067)
XLA Ops:
  0.0 69.4 %shard_map.46 = f32[64,64]{1,0:T(8,128)S(1)} custom-call(bf16[1024,1792]{1,0:T(8,128)(2,1)} %act.1, bf16[1024,512]{1,0:T(8,128)(2,1)} %og.1, bf16[4,64,1792]{2,1,0:T(8,128)(2,1)} %bitcast.2, bf16[4,64,512]{2,1,0:T(8,128)(2,1)} %bitcast.3), custom_call_target="tpu_custom_call" | custom-call | tf_op jit(solution)/shard_map/pallas_call | solution.py:459
  69.4 0.6 copy.6

commit v5 on v4

--- a/solution.py
+++ b/solution.py
@@ -45,6 +45,10 @@
 def last_groups(k):
     third, fourth = order_of(k)[2:]
     return [8 >> third, 8 >> fourth, (8 >> third) + (8 >> fourth)]
+
+
+def streams_at(level):
+    return sorted(range(STREAMS), key=lambda k: order_of(k)[level] % 2)
 
 
 def rows_at(group, k):
@@ -272,8 +276,8 @@
         n = 128 >> level
         m = n // 2
         slot = step % SLOTS
-        scales = []
-        for k in range(STREAMS):
+        scales = {}
+        for k in streams_at(level):
             message(step, level, k).wait()
             theirs = recvs[level][step, k, pl.ds(4 * n, 16), :].astype(F32)
             scale, inverse, fresh = [], [], []
@@ -290,7 +294,7 @@
                     total = total_of(step, level, k, ct, group, scale[ct // 2])
                     sends[level + 1][step, k, pl.ds(ct * m + i * 16, 16), :] = rows_of(encode(total, inverse[ct // 2]))
             message(step, level + 1, k).start()
-            scales.append(scale)
+            scales[k] = scale
         for k in range(STREAMS):
             for ct in range(4):
                 for group in split(k, level + 1)[1]:
@@ -327,8 +331,8 @@
 
     def spread(step):
         level, slot = 1, step % SLOTS
-        scales = []
-        for k in range(STREAMS):
+        scales = {}
+        for k in streams_at(level):
             message(step, level, k).wait()
             theirs = recvs[level][step, k, pl.ds(4 * 64, 16), :].astype(F32)
             scale, inverse, fresh = next_bounds(step, k, theirs)
@@ -338,7 +342,7 @@
                     total = total_of(step, level, k, ct, group, scale[ct // 2])
                     ds[step - DIRECT, k, j, pl.ds(ct * 16, 16), :] = rows_of(encode(total, inverse[ct // 2]))
                 direct(step, k, j).start()
-            scales.append(scale)
+            scales[k] = scale
         for k in range(STREAMS):
             for ct in range(4):
                 total = total_of(step, level, k, ct, 0, scales[k][ct // 2])

time: 70.1 us -> 69.5 us (level)
  no operation moved by 1% of the time
where the time goes in v5:
time: 69.5 us; the launch traced here: 69.4 us
  Pallas kernels  68.8 us (99%)
    pallas_call x1, Pallas kernels, shards(): pl.pallas_call(kernel, out_shape=pltpu.VMEM((64, 64), F32), in_specs=[pl....  68.8 us

profile of v5, /device:TPU:0, one launch (start us, length us, event | category | flops | bytes accessed | tf_op | source)
XLA Modules:
  0.0 69.4 jit_solution(2564798420356604531)
XLA Ops:
  0.0 68.8 %shard_map.46 = f32[64,64]{1,0:T(8,128)S(1)} custom-call(bf16[1024,1792]{1,0:T(8,128)(2,1)} %act.1, bf16[1024,512]{1,0:T(8,128)(2,1)} %og.1, bf16[4,64,1792]{2,1,0:T(8,128)(2,1)} %bitcast.2, bf16[4,64,512]{2,1,0:T(8,128)(2,1)} %bitcast.3), custom_call_target="tpu_custom_call" | custom-call | tf_op jit(solution)/shard_map/pallas_call | solution.py:463
  68.8 0.6 copy.6

commit v6 on v5

--- a/solution.py
+++ b/solution.py
@@ -313,10 +313,13 @@
         quarter = jnp.where(near, step - 2, 2 * (step % 2) + block % 2)
         quarter = jnp.where(step < 2, block, quarter)
         query = chip * 16 + side * 8 + quarter * 2 + (row % 64) // RANK
-        return jnp.where(query == column, 1.0, 0.0).astype(F32)
+        return jnp.where(query == column, 1.0, 0.0).astype(BF16)
 
     def add_scores(choice):
-        sums = jnp.dot(prod[...], choice, precision=lax.Precision.HIGHEST, preferred_element_type=F32)
+        values = prod[...]
+        high = values.astype(BF16)
+        low = (values - high.astype(F32)).astype(BF16)
+        sums = jnp.dot(high, choice, preferred_element_type=F32) + jnp.dot(low, choice, preferred_element_type=F32)
         out[...] += sums * RANK**-0.5
 
     def next_bounds(step, k, theirs):
@@ -362,16 +365,19 @@
 
     def finish_direct(step):
         choice = choice_of(step)
-        for k in range(STREAMS):
-            total = [tiles(part[step % SLOTS, ct, rows_at(0, k), :]) for ct in range(4)]
-            for j in range(3):
+        total = {
+            (k, ct): tiles(part[step % SLOTS, ct, rows_at(0, k), :]) for k in range(STREAMS) for ct in range(4)
+        }
+        for j in range(3):
+            for k in range(STREAMS):
                 direct(step, k, j).wait()
                 theirs = dr[step - DIRECT, k, j, pl.ds(64, 16), :].astype(F32)
                 scale = [theirs[:8] * (1.0 / TOP), theirs[8:] * (1.0 / TOP)]
                 for ct in range(4):
-                    total[ct] += decode(tiles(dr[step - DIRECT, k, j, pl.ds(ct * 16, 16), :]), scale[ct // 2])
+                    total[k, ct] += decode(tiles(dr[step - DIRECT, k, j, pl.ds(ct * 16, 16), :]), scale[ct // 2])
+        for k in range(STREAMS):
             for c in range(2):
-                prod[pl.ds(k * 16, 16), pl.ds(c * 128, 128)] = rows_of(total[c] * total[2 + c])
+                prod[pl.ds(k * 16, 16), pl.ds(c * 128, 128)] = rows_of(total[k, c] * total[k, 2 + c])
         add_scores(choice)
 
     out[...] = jnp.zeros_like(out)

time: 69.5 us -> 69.3 us (level)
  no operation moved by 1% of the time
where the time goes in v6:
time: 69.3 us; the launch traced here: 69.2 us
  Pallas kernels  68.6 us (99%)
    pallas_call x1, Pallas kernels, shards(): pl.pallas_call(kernel, out_shape=pltpu.VMEM((64, 64), F32), in_specs=[pl....  68.6 us

profile of v6, /device:TPU:0, one launch (start us, length us, event | category | flops | bytes accessed | tf_op | source)
XLA Modules:
  0.0 69.2 jit_solution(7759604970822766859)
XLA Ops:
  0.0 68.6 %shard_map.46 = f32[64,64]{1,0:T(8,128)S(1)} custom-call(bf16[1024,1792]{1,0:T(8,128)(2,1)} %act.1, bf16[1024,512]{1,0:T(8,128)(2,1)} %og.1, bf16[4,64,1792]{2,1,0:T(8,128)(2,1)} %bitcast.2, bf16[4,64,512]{2,1,0:T(8,128)(2,1)} %bitcast.3), custom_call_target="tpu_custom_call" | custom-call | tf_op jit(solution)/shard_map/pallas_call | solution.py:469
  68.6 0.6 copy.6

commit v7 on v6

--- a/solution.py
+++ b/solution.py
@@ -237,11 +237,15 @@
         @pl.when(step == 0)
         def _():
             pltpu.make_async_copy(og, g_v, load_sem.at[1]).wait()
-            pltpu.make_async_copy(act, a_v, load_sem.at[0]).wait()
 
     def multiply(step):
         slot = step % SLOTS
-        for t, (tokens, queries) in enumerate(((a_v, qi_v), (g_v, qo_v))):
+        for t, tokens, queries in ((1, g_v, qo_v), (0, a_v, qi_v)):
+            if t == 0:
+                @pl.when(step == 0)
+                def _():
+                    pltpu.make_async_copy(act, a_v, load_sem.at[0]).wait()
+
             weights = queries[step].reshape(256, queries.shape[3])
             for m in range(2):
                 block = lax.dot_general(

time: 69.3 us -> 69.6 us (level)
  no operation moved by 1% of the time
where the time goes in v7:
time: 69.6 us; the launch traced here: 69.5 us
  Pallas kernels  68.8 us (99%)
    pallas_call x1, Pallas kernels, shards(): pl.pallas_call(kernel, out_shape=pltpu.VMEM((64, 64), F32), in_specs=[pl....  68.8 us

profile of v7, /device:TPU:0, one launch (start us, length us, event | category | flops | bytes accessed | tf_op | source)
XLA Modules:
  0.0 69.5 jit_solution(2489210723579103460)
XLA Ops:
  0.0 68.8 %shard_map.46 = f32[64,64]{1,0:T(8,128)S(1)} custom-call(bf16[1024,1792]{1,0:T(8,128)(2,1)} %act.1, bf16[1024,512]{1,0:T(8,128)(2,1)} %og.1, bf16[4,64,1792]{2,1,0:T(8,128)(2,1)} %bitcast.2, bf16[4,64,512]{2,1,0:T(8,128)(2,1)} %bitcast.3), custom_call_target="tpu_custom_call" | custom-call | tf_op jit(solution)/shard_map/pallas_call | solution.py:473
  68.9 0.6 copy.6
